TPU v7x, 128 devices: a whole 4x4x4 slice. The times are simulated.
128 devices in a mesh: seq: 32 (over z, x, core), head: 4 (over y).
Axes of the slice: x: 4, y: 4, z: 4, core: 2. Of those that a mesh axis runs over, the one named last changes fastest.
Arguments:
- qkv: bfloat16 [3, 32768, 40, 128], P(None, 'seq', 'head'), may hold values from -200 to 200
- head_type: int32 [40], P('head'), may hold values from 0 to 1, as said below
- out_weight: bfloat16 [40, 128, 5120], P('head'), may hold values from -0.5 to 0.5
Outputs:
- mixed: bfloat16 [32768, 5120], P(('seq', 'head'))
Inputs may be any that keep to these rules, and one draw needn't show every extreme that they name: `head_type`: in each block of 10 consecutive heads exactly 5 heads are temporal (1), the others spatial (0).
All inputs are finite; a program needn't handle non-finite values.
Results may differ from a plain program's by a relative error of at most 0.02.
Values may be sent and summed in bfloat16 or wider, within the bound.
A program may use at most 128 MiB of HBM per device.

v0:
```python
import jax
import jax.numpy as jnp
from jax import lax
from jax.sharding import PartitionSpec as P


def attend(query_matrix, key_matrix, value_matrix, softmax_scale):
    attention_logits = (
        jnp.einsum("gnz,gcz->gnc", query_matrix, key_matrix, preferred_element_type=jnp.float32)
        * softmax_scale
    )
    highest = jnp.max(attention_logits, axis=-1, keepdims=True)
    weights = jnp.exp(attention_logits - highest)
    summed = jnp.sum(weights, axis=-1, keepdims=True)
    attention_probs = (weights / summed).astype(jnp.bfloat16)
    attended_output = jnp.einsum(
        "clg,cgz->clz", attention_probs, value_matrix, preferred_element_type=jnp.float32
    )
    return attended_output.astype(jnp.bfloat16)


def across_frames(arrived, softmax_scale):
    frame_count, place_count, head_count, width = arrived.shape[1:]
    arranged = jnp.transpose(arrived, (0, 2, 3, 1, 4)).reshape(
        3, place_count * head_count, frame_count, width
    )
    attended_output = attend(arranged[0], arranged[1], arranged[2], softmax_scale)
    attended_output = attended_output.reshape(place_count, head_count, frame_count, width)
    return jnp.transpose(attended_output, (2, 0, 1, 3))


def shards(qkv, head_type, out_weight):
    tokens_here = qkv.shape[1]
    heads_here = qkv.shape[2]
    width = qkv.shape[3]
    temp_count = heads_here // 2
    space_count = heads_here - temp_count
    softmax_scale = width ** (-0.5)
    ranking = jnp.argsort(head_type, stable=True)
    spatial_heads = jnp.take(qkv, ranking[:space_count], axis=2)
    temporal_heads = jnp.take(qkv, ranking[space_count:], axis=2)
    block_rows = min(512, tokens_here)
    block_count = tokens_here // block_rows
    key_matrix = jnp.transpose(spatial_heads[1], (1, 0, 2))
    value_matrix = jnp.transpose(spatial_heads[2], (1, 0, 2))
    query_blocks = jnp.transpose(
        spatial_heads[0].reshape(block_count, block_rows, space_count, width), (0, 2, 1, 3)
    )
    spatial_out = lax.map(
        lambda query_block: attend(query_block, key_matrix, value_matrix, softmax_scale),
        query_blocks,
    )
    spatial_out = jnp.transpose(spatial_out, (0, 2, 1, 3)).reshape(tokens_here, space_count, width)
    sectioned = temporal_heads.reshape(3, 1, tokens_here, temp_count, width)
    arrived = lax.all_to_all(sectioned, "seq", split_axis=2, concat_axis=1, tiled=True)
    attended_output = across_frames(arrived, softmax_scale)
    returned = lax.all_to_all(attended_output, "seq", split_axis=0, concat_axis=1, tiled=True)
    temporal_out = returned.reshape(tokens_here, temp_count, width)
    combined = jnp.concatenate([spatial_out, temporal_out], axis=1).reshape(
        tokens_here, heads_here * width
    )
    sorted_weight = jnp.take(out_weight, ranking, axis=0).reshape(
        heads_here * width, out_weight.shape[2]
    )
    return lax.psum_scatter(
        jnp.dot(combined, sorted_weight, preferred_element_type=jnp.float32).astype(jnp.bfloat16),
        "head",
        scatter_dimension=0,
        tiled=True,
    )


def solution(mesh):
    in_specs = (P(None, "seq", "head", None), P("head"), P("head", None, None))
    out_specs = P(("seq", "head"), None)
    return jax.shard_map(shards, mesh=mesh, in_specs=in_specs, out_specs=out_specs, check_vma=False)
```

profile of v0, /device:TPU:1, one launch (start us, length us, event | category | flops | bytes accessed | tf_op | source)
XLA Modules:
  0.0 285.7 jit_solution(3001595454272910843)
XLA Ops:
  6.5 1.9 sort.17
  8.4 0.1 compare_and_fusion.1
  8.5 6.4 %gather_fusion.2 = bf16[5,3,1024,128]{3,2,1,0:T(8,128)(2,1)} fusion(bf16[3,1024,10,128]{3,1,2,0:T(8,128)(2,1)} %param.7, s32[1024]{0:T(1024)S(1)} %pad_clamp_fusion.1), kind=kCustom, calls=%fused_computation.1.clone | custom fusion | bytes 7864340 | tf_op jit(solution)/shard_map/jit(_take)/gather | solution.py:41
  14.9 2.6 select_bitcast_fusion
  17.5 5.7 %copy.29 = bf16[3,1,1024,5,128]{4,0,3,1,2:T(4,128)(2,1)} copy(bf16[3,1,1024,5,128]{4,2,0,3,1:T(8,128)(2,1)S(1)} %select_bitcast_fusion) | data formatting | bytes 7864320 | tf_op jit(solution)/shard_map/reshape | solution.py:54
  23.2 9.5 %all-to-all-start = ((bf16[3,1,1024,5,128]{4,0,3,1,2:T(4,128)(2,1)}), bf16[3,1,1024,5,128]{4,0,3,1,2:T(4,128)(2,1)}, u32[]{:S(2)}, u32[]{:S(2)}) async-start(bf16[3,1,1024,5,128]{4,0,3,1,2:T(4,128)(2,1)} %copy.29), calls=%async_computation | async-start | bytes 10485760 | tf_op jit(solution)/shard_map/all_to_all | solution.py:55
  32.7 6.5 %gather_fusion.1 = bf16[5,3,1024,128]{3,2,1,0:T(8,128)(2,1)} fusion(bf16[3,1024,10,128]{3,1,2,0:T(8,128)(2,1)} %param.7, s32[1024]{0:T(1024)S(1)} %pad_clamp_fusion.2), kind=kCustom, calls=%fused_computation.clone | custom fusion | bytes 7864340 | tf_op jit(solution)/shard_map/jit(_take)/gather | solution.py:40
  39.2 2.6 select_bitcast_fusion.1
  41.8 1.8 slice_bitcast_fusion
  43.5 0.1 copy.40
  43.6 50.5 %all-to-all-done = bf16[3,1,1024,5,128]{4,0,3,1,2:T(4,128)(2,1)} async-done(((bf16[3,1,1024,5,128]{4,0,3,1,2:T(4,128)(2,1)}), bf16[3,1,1024,5,128]{4,0,3,1,2:T(4,128)(2,1)}, u32[]{:S(2)}, u32[]{:S(2)}) %all-to-all-start) | async-done | bytes 3932192 | tf_op jit(solution)/shard_map/all_to_all | solution.py:55
  94.2 5.7 %copy.38 = bf16[3,32,32,5,128]{4,1,3,2,0:T(8,128)(2,1)S(1)} copy(bf16[3,32,32,5,128]{4,0,3,2,1:T(4,128)(2,1)} %bitcast.13) | data formatting | bytes 7864320 | tf_op jit(solution)/shard_map/all_to_all | solution.py:55
  99.9 2.2 fusion.52
  102.1 4.3 %fusion.53 = (f32[160,32]{1,0:T(8,128)S(1)}, f32[160,32,32]{1,2,0:T(8,128)}) fusion(bf16[160,32,128]{2,1,0:T(8,128)(2,1)} %bitcast.76, bf16[160,32,128]{2,1,0:T(8,128)(2,1)} %bitcast.75), kind=kOutput, calls=%fused_computation.60 | convolution fusion | flops 42434592 | bytes 3297280 | tf_op jit(solution)/shard_map/sub | solution.py:13
  106.4 2.4 convolution_convert_fusion
  108.7 1.6 copy.39
  110.3 8.2 %all-to-all-start.1 = ((bf16[32,32,5,128]{3,1,2,0:T(8,128)(2,1)}), bf16[32,32,5,128]{3,1,2,0:T(8,128)(2,1)S(1)}, u32[]{:S(2)}, u32[]{:S(2)}) async-start(bf16[32,32,5,128]{3,1,2,0:T(8,128)(2,1)} %bitcast.57), calls=%async_computation.1 | async-start | bytes 2621440 | tf_op jit(solution)/shard_map/all_to_all | solution.py:57
  118.5 0.3 reduce-scatter.2.cloned.1.call-start
  118.7 30.4 %while.10 = (s32[]{:T(128)}, bf16[2,5,512,128]{3,2,1,0:T(8,128)(2,1)}, bf16[2,5,512,128]{3,2,1,0:T(8,128)(2,1)S(1)}, bf16[5,1024,128]{2,1,0:T(8,128)(2,1)}, bf16[5,1024,128]{2,1,0:T(8,128)(2,1)}, /*index=5*/s32[]{:T(128)}) while((s32[]{:T(128)}, bf16[2,5,512,128]{3,2,1,0:T(8,128)(2,1)}, bf16[2,5,512,128]{3,2,1,0:T(8,128)(2,1)S(1)}, ...), condition=%wide.region_4.6_spmd, body=%wide.region_1.5_spmd.sunk | while | flops 1355613184 | bytes 24924244 | solution.py:49
  118.8 8.5 %fusion.70 = (f32[5,512]{1,0:T(8,128)S(1)}, f32[5,512,1024]{2,1,0:T(8,128)}) fusion(bf16[5,1024,128]{2,1,0:T(8,128)(2,1)} %get-tuple-element.112, bf16[2,5,512,128]{3,2,1,0:T(8,128)(2,1)S(1)} %get-tuple-element.111, s32[]{:T(128)S(6)} %copy.44), kind=kOutput, calls=%fused_computation.58.clone.1 | convolution fusion | flops 678953984 | bytes 12462084 | tf_op jit(solution)/shard_map/while/body/eval_jaxpr/sub | solution.py:13
  127.2 6.7 %fusion.71 = bf16[2,5,512,128]{3,2,1,0:T(8,128)(2,1)} fusion(bf16[2,5,512,128]{3,2,1,0:T(8,128)(2,1)} %get-tuple-element.104, s32[]{:T(128)S(6)} %copy.44, bf16[5,1024,128]{2,1,0:T(8,128)(2,1)} %get-tuple-element.113, f32[5,512,1024]{2,1,0:T(8,128)} %get-tuple-element.95, f32[5,512]{1,0:T(8,128)S(1)} %get-tuple-element.96), kind=kOutput, calls=%fused_computation.12.clone.1 | convolution fusion | flops 676659200 | bytes 12462084 | tf_op jit(solution)/shard_map/while/body/eval_jaxpr/clg,cgz->clz/dot_general | solution.py:16
  133.9 8.4 %fusion.70 = (f32[5,512]{1,0:T(8,128)S(1)}, f32[5,512,1024]{2,1,0:T(8,128)}) fusion(bf16[5,1024,128]{2,1,0:T(8,128)(2,1)} %get-tuple-element.112, bf16[2,5,512,128]{3,2,1,0:T(8,128)(2,1)S(1)} %get-tuple-element.111, s32[]{:T(128)S(6)} %copy.44), kind=kOutput, calls=%fused_computation.58.clone.1 | convolution fusion | flops 678953984 | bytes 12462084 | tf_op jit(solution)/shard_map/while/body/eval_jaxpr/sub | solution.py:13
  142.4 6.7 %fusion.71 = bf16[2,5,512,128]{3,2,1,0:T(8,128)(2,1)} fusion(bf16[2,5,512,128]{3,2,1,0:T(8,128)(2,1)} %get-tuple-element.104, s32[]{:T(128)S(6)} %copy.44, bf16[5,1024,128]{2,1,0:T(8,128)(2,1)} %get-tuple-element.113, f32[5,512,1024]{2,1,0:T(8,128)} %get-tuple-element.95, f32[5,512]{1,0:T(8,128)S(1)} %get-tuple-element.96), kind=kOutput, calls=%fused_computation.12.clone.1 | convolution fusion | flops 676659200 | bytes 12462084 | tf_op jit(solution)/shard_map/while/body/eval_jaxpr/clg,cgz->clz/dot_general | solution.py:16
  149.1 1.4 copy.28
  150.6 11.0 %gather_fusion = bf16[10,128,5120]{2,1,0:T(8,128)(2,1)} fusion(bf16[10,128,5120]{2,1,0:T(8,128)(2,1)} %param.9, s32[1024]{0:T(1024)S(1)} %pad_clamp_fusion), kind=kCustom, calls=%fused_computation.2 | custom fusion | bytes 26214440 | tf_op jit(solution)/shard_map/jit(_take)/gather | solution.py:62
  161.6 0.0 all-to-all-done.1
  161.6 0.3 copy.33
  161.9 18.0 %bitcast_convert_fusion = bf16[1024,5120]{1,0:T(8,128)(2,1)} fusion(bf16[10,128,5120]{2,1,0:T(8,128)(2,1)} %gather_fusion, pred[10]{0:T(512)(128)(4,1)S(1)} %compare_and_fusion.2, bf16[1024,5,128]{2,0,1:T(8,128)(2,1)S(1)} %bitcast.72, bf16[1024,5,128]{2,0,1:T(8,128)(2,1)S(1)} %bitcast.71), kind=kOutput, calls=%fused_computation.23 | convolution fusion | flops 13434880000 | bytes 26214410 | tf_op jit(solution)/shard_map/dot_general | solution.py:66
  179.9 0.0 reduce-scatter.2.cloned.1.call-update
  179.9 99.0 %reduce-scatter.2.cloned.1.call-done = bf16[256,5120]{1,0:T(8,128)(2,1)} async-done(((bf16[1024,5120]{1,0:T(8,128)(2,1)}), bf16[256,5120]{1,0:T(8,128)(2,1)}) %reduce-scatter.2.cloned.1.call-update) | async-done | bytes 2621456 | tf_op jit(solution)/shard_map/reduce_scatter | solution.py:65
  (7 shorter events, 0.0 us)
Async XLA Ops:
  23.2 71.0 %all-to-all-start = ((bf16[3,1,1024,5,128]{4,0,3,1,2:T(4,128)(2,1)}), bf16[3,1,1024,5,128]{4,0,3,1,2:T(4,128)(2,1)}, u32[]{:S(2)}, u32[]{:S(2)}) async-start(bf16[3,1,1024,5,128]{4,0,3,1,2:T(4,128)(2,1)} %copy.29), calls=%async_computation | async-start | bytes 10485760 | tf_op jit(solution)/shard_map/all_to_all | solution.py:55
  110.3 51.3 %all-to-all-start.1 = ((bf16[32,32,5,128]{3,1,2,0:T(8,128)(2,1)}), bf16[32,32,5,128]{3,1,2,0:T(8,128)(2,1)S(1)}, u32[]{:S(2)}, u32[]{:S(2)}) async-start(bf16[32,32,5,128]{3,1,2,0:T(8,128)(2,1)} %bitcast.57), calls=%async_computation.1 | async-start | bytes 2621440 | tf_op jit(solution)/shard_map/all_to_all | solution.py:57
  118.5 160.4 %reduce-scatter.2.cloned.1.call-start = ((), (), s32[]{:S(2)}) async-start(), calls=%async_computation.3 | async-start | bytes 13107200 | tf_op jit(solution)/shard_map/reduce_scatter | solution.py:65
Sparse Core Ops, SparseCore 0:
  180.0 98.8 reduce-scatter.1
where the time goes:
time: 286 us
  waiting for transfers between devices  150 us (52%)
  matrix products  55 us (19%)
  local copies, waits for them, and re-layouts  42.7 us (15%)
  starting transfers between devices  17.9 us (6%)
  between operations  13.5 us (5%)
  other arithmetic  7.11 us (2%)
    reduce_scatter x1, waiting for transfers between devices, shards(): lax.psum_scatter(jnp.dot(combined, sorted_weight, preferred_element_type=...  99 us
    all_to_all x1, waiting for transfers between devices, shards(): lax.all_to_all(sectioned, 'seq', split_axis=2, concat_axis=1, tiled=True)  50.5 us
    sub x3, matrix products, attend(): weights = jnp.exp(attention_logits - highest)  21.2 us
    dot_general x1, matrix products, shards(): jnp.dot(combined, sorted_weight, preferred_element_type=jnp.float32)  18 us
    dot_general x3, matrix products, attend(): jnp.einsum('clg,cgz->clz', attention_probs, value_matrix, preferred_eleme...  15.8 us
    gather x1, local copies, waits for them, and re-layouts, shards(): jnp.take(out_weight, ranking, axis=0)  11 us
    all_to_all x1, starting transfers between devices, shards(): lax.all_to_all(sectioned, 'seq', split_axis=2, concat_axis=1, tiled=True)  9.49 us
    all_to_all x1, starting transfers between devices, shards(): lax.all_to_all(attended_output, 'seq', split_axis=0, concat_axis=1, tiled...  8.16 us
  transfers between devices with their start and end apart: 3, of which 2 were waited for; matrix products, arithmetic and copies ran while one was open for 19% of the time, Pallas kernels for 0%

commit v1 on v0

v1 whole, which is shorter than its diff:
```python
import functools

import jax
import jax.numpy as jnp
from jax import lax
from jax.experimental import pallas as pl
from jax.experimental.pallas import tpu as pltpu
from jax.sharding import PartitionSpec as P

MESH = pl.DeviceIdType.MESH
BLOCK = 16
CHUNKS = 4
NEG = -1e30


def softmax_times(scores, values, factor):
    highest = jnp.max(scores, axis=-1, keepdims=True)
    weights = jnp.exp2((scores - highest) * factor)
    total = jnp.sum(weights, axis=-1, keepdims=True)
    mixed = jnp.dot(weights.astype(jnp.bfloat16), values, preferred_element_type=jnp.float32)
    return (mixed / total).astype(jnp.bfloat16)


def scores_of(queries, keys):
    return lax.dot_general(queries, keys, (((1,), (1,)), ((), ())), preferred_element_type=jnp.float32)


def kernel(
    n_seq, n_head, chunks, kind_ref, qkv_hbm, weight_hbm, out_hbm,
    qkv, weight, packed, arrived, answers, returned, attended, partial, passing, order,
    qkv_sem, weight_sem, there_send, there_recv, back_send, back_recv, ring_send, ring_recv, out_sem,
):
    heads, tokens, width = qkv.shape[1:]
    half = heads // 2
    dests = tokens // BLOCK // chunks
    stride = n_seq // dests
    rows = tokens // n_head // chunks
    per_owner = rows // BLOCK
    share = tokens // n_head
    columns = weight.shape[2] // 2
    factor = width**-0.5 * 1.4426950408889634
    s = lax.axis_index("seq")
    g = lax.axis_index("head")
    right, left = lax.rem(g + 1, n_head), lax.rem(g + n_head - 1, n_head)
    side = (right, left)

    qkv_copy = pltpu.make_async_copy(qkv_hbm, qkv, qkv_sem)
    qkv_copy.start()
    weight_copy = pltpu.make_async_copy(weight_hbm, weight, weight_sem)

    barrier = pltpu.get_barrier_semaphore()

    def greet(i, _):
        pl.semaphore_signal(barrier, inc=1, device_id={"seq": lax.rem(s + i, n_seq), "head": g}, device_id_type=MESH)
        return 0

    lax.fori_loop(1, n_seq, greet, 0)
    for y in side:
        pl.semaphore_signal(barrier, inc=1, device_id={"seq": s, "head": y}, device_id_type=MESH)

    found = [jnp.int32(0), jnp.int32(0)]
    listed = [jnp.int32(0)] * heads
    for i in range(heads):
        temporal = kind_ref[i] == 1
        place = jnp.where(temporal, found[1] + half, found[0])
        for j in range(heads):
            listed[j] = jnp.where(place == j, jnp.int32(i), listed[j])
        found[0] = found[0] + jnp.where(temporal, 0, 1)
        found[1] = found[1] + jnp.where(temporal, 1, 0)
    for j in range(heads):
        order[j] = listed[j]

    qkv_copy.wait()
    weight_copy.start()

    def pack(i, _):
        packed[i] = qkv[i // half, order[half + lax.rem(i, half)]]
        return 0

    lax.fori_loop(0, 3 * half, pack, 0)
    pl.semaphore_wait(barrier, n_seq - 1 + 2)

    def is_dest(c):
        return lax.rem(s, stride) == lax.rem(c, stride)

    def send_there(c):
        slot = c // stride

        def one(i, _):
            j = lax.rem(i + s // stride, dests)
            to = j * stride + lax.rem(c, stride)
            first = pl.multiple_of(share * (j // per_owner) + rows * c + BLOCK * lax.rem(j, per_owner), BLOCK)
            src = packed.at[:, pl.ds(first, BLOCK), :]
            dst = arrived.at[slot, s]

            @pl.when(to == s)
            def _():
                pltpu.make_async_copy(src, dst, there_recv.at[slot]).start()

            @pl.when(to != s)
            def _():
                pltpu.make_async_remote_copy(
                    src_ref=src, dst_ref=dst, send_sem=there_send.at[c], recv_sem=there_recv.at[slot],
                    device_id={"seq": to, "head": g}, device_id_type=MESH,
                ).start()

            return 0

        lax.fori_loop(0, dests, one, 0)

    def temporal_part(c):
        slot = c // stride
        block = s // stride

        @pl.when(is_dest(c))
        def _():
            pltpu.make_async_copy(arrived.at[slot], arrived.at[slot], there_recv.at[slot]).wait()
            n = n_seq * BLOCK
            piece = n // 2
            same = lax.rem(lax.broadcasted_iota(jnp.int32, (piece, n), 0), BLOCK) == lax.rem(
                lax.broadcasted_iota(jnp.int32, (piece, n), 1), BLOCK
            )
            for h in range(half):
                keys = arrived[slot, :, half + h].reshape(n, width)
                values = arrived[slot, :, 2 * half + h].reshape(n, width)
                for p in range(2):
                    of = pl.ds(p * (n_seq // 2), n_seq // 2)
                    queries = arrived[slot, of, h].reshape(piece, width)
                    scores = jnp.where(same, scores_of(queries, keys), NEG)
                    answers[slot, of, h] = softmax_times(scores, values, factor).reshape(n_seq // 2, BLOCK, width)

            def one(i, _):
                to = lax.rem(i + s, n_seq)
                src = answers.at[slot, to]
                dst = returned.at[c, block]

                @pl.when(to == s)
                def _():
                    pltpu.make_async_copy(src, dst, back_recv.at[c]).start()

                @pl.when(to != s)
                def _():
                    pltpu.make_async_remote_copy(
                        src_ref=src, dst_ref=dst, send_sem=back_send.at[slot], recv_sem=back_recv.at[c],
                        device_id={"seq": to, "head": g}, device_id_type=MESH,
                    ).start()

                return 0

            lax.fori_loop(0, n_seq, one, 0)

    def spatial_part(c):
        slot = lax.rem(c, 2)
        for h in range(half):
            head = order[h]
            queries = jnp.concatenate(
                [qkv[0, head, pl.ds(pl.multiple_of(share * o + rows * c, BLOCK), rows), :] for o in range(n_head)], axis=0
            )
            attended[slot, :, h * width : (h + 1) * width] = softmax_times(
                scores_of(queries, qkv[1, head]), qkv[2, head], factor
            )

    def project(c):
        slot = lax.rem(c, 2)
        pltpu.make_async_copy(returned.at[c], returned.at[c], back_recv.at[c]).wait()
        for h in range(half):
            attended[slot, :, (half + h) * width : (half + h + 1) * width] = returned[c, :, h].reshape(
                n_head * rows, width
            )
        tile = 512 if columns % 512 == 0 else columns
        for d in range(2):
            for t in range(columns // tile):
                cols = slice(d * columns + t * tile, d * columns + (t + 1) * tile)
                total = None
                for k in range(half):
                    pair = jnp.concatenate([weight[order[2 * k], :, cols], weight[order[2 * k + 1], :, cols]], axis=0)
                    term = jnp.dot(
                        attended[slot, :, 2 * k * width : 2 * (k + 1) * width], pair, preferred_element_type=jnp.float32
                    )
                    total = term if total is None else total + term
                partial[c, d, :, :, t * tile : (t + 1) * tile] = total.astype(jnp.bfloat16).reshape(n_head, rows, tile)

    def ring_copy(c, d, t):
        if t == 0:
            owner = lax.rem(g + (n_head - 1 if d == 0 else 1), n_head)
            src = partial.at[c, d, owner]
        else:
            src = passing.at[c, d, t - 1]
        return pltpu.make_async_remote_copy(
            src_ref=src, dst_ref=passing.at[c, d, t], send_sem=ring_send.at[c, d, t], recv_sem=ring_recv.at[c, d, t],
            device_id={"seq": s, "head": side[d]}, device_id_type=MESH,
        )

    def add_own(c, d, t):
        owner = lax.rem(g + (2 * n_head - 2 - t if d == 0 else 2 + t), n_head)
        passing[c, d, t] = (passing[c, d, t].astype(jnp.float32) + partial[c, d, owner].astype(jnp.float32)).astype(
            jnp.bfloat16
        )

    def ring_step(c, t):
        for d in range(2):
            ring_copy(c, d, t).wait_recv()
            add_own(c, d, t)
            ring_copy(c, d, t + 1).start()

    def out_copy(c, d):
        return pltpu.make_async_copy(
            passing.at[c, d, n_head - 2],
            out_hbm.at[pl.ds(pl.multiple_of(rows * c, BLOCK), rows), pl.ds(d * columns, columns)],
            out_sem.at[c, d],
        )

    def ring_end(c):
        for d in range(2):
            ring_copy(c, d, n_head - 2).wait_recv()
            add_own(c, d, n_head - 2)
            out_copy(c, d).start()

    def when_in(c, what):
        @pl.when(jnp.logical_and(c >= 0, c < chunks))
        def _():
            what(c)

    send_there(jnp.int32(0))
    send_there(jnp.int32(1))
    spatial_part(jnp.int32(0))
    temporal_part(jnp.int32(0))
    weight_copy.wait()

    def tick(k, _):
        when_in(k - n_head + 1, ring_end)
        for t in range(n_head - 3, -1, -1):
            when_in(k - 1 - t, functools.partial(ring_step, t=t))

        def start(c):
            project(c)
            for d in range(2):
                ring_copy(c, d, 0).start()

        when_in(k + 2, send_there)
        when_in(k + 1, spatial_part)
        when_in(k, start)
        when_in(k + 1, temporal_part)
        return 0

    lax.fori_loop(0, chunks + n_head - 1, tick, 0)

    def finish(c, _):
        for d in range(2):
            for t in range(n_head - 1):
                ring_copy(c, d, t).wait_send()
            out_copy(c, d).wait()

        @pl.when(is_dest(c))
        def _():
            few = packed.at[:, pl.ds(0, BLOCK * (dests - 1)), :]
            pltpu.make_async_copy(few, few, there_send.at[c]).wait()
            slot = c // stride
            most = answers.at[slot, pl.ds(0, n_seq - 1)]
            pltpu.make_async_copy(most, most, back_send.at[slot]).wait()

        @pl.when(jnp.logical_not(is_dest(c)))
        def _():
            all_ = packed.at[:, pl.ds(0, BLOCK * dests), :]
            pltpu.make_async_copy(all_, all_, there_send.at[c]).wait()

        return 0

    lax.fori_loop(0, chunks, finish, 0)


def shards(n_seq, n_head, chunks, qkv, head_type, out_weight):
    kinds, tokens, heads, width = qkv.shape
    model = out_weight.shape[2]
    half = heads // 2
    dests = tokens // BLOCK // chunks
    slots = chunks * dests // n_seq
    rows = tokens // n_head // chunks
    bf16 = jnp.bfloat16
    dma = pltpu.SemaphoreType.DMA
    any_ = pl.BlockSpec(memory_space=pl.ANY)
    return pl.pallas_call(
        functools.partial(kernel, n_seq, n_head, chunks),
        out_shape=jax.ShapeDtypeStruct((tokens // n_head, model), bf16),
        in_specs=[pl.BlockSpec(memory_space=pltpu.SMEM), any_, any_],
        out_specs=any_,
        scratch_shapes=[
            pltpu.VMEM((3, heads, tokens, width), bf16),
            pltpu.VMEM((heads, width, model), bf16),
            pltpu.VMEM((3 * half, tokens, width), bf16),
            pltpu.VMEM((slots, n_seq, 3 * half, BLOCK, width), bf16),
            pltpu.VMEM((slots, n_seq, half, BLOCK, width), bf16),
            pltpu.VMEM((chunks, dests, half, BLOCK, width), bf16),
            pltpu.VMEM((2, n_head * rows, heads * width), bf16),
            pltpu.VMEM((chunks, 2, n_head, rows, model // 2), bf16),
            pltpu.VMEM((chunks, 2, n_head - 1, rows, model // 2), bf16),
            pltpu.SMEM((heads,), jnp.int32),
            dma,
            dma,
            dma((chunks,)),
            dma((slots,)),
            dma((slots,)),
            dma((chunks,)),
            dma((chunks, 2, n_head - 1)),
            dma((chunks, 2, n_head - 1)),
            dma((chunks, 2)),
        ],
        compiler_params=pltpu.CompilerParams(
            collective_id=0, has_side_effects=True, vmem_limit_bytes=62 * 1024 * 1024
        ),
        cost_estimate=pl.CostEstimate(flops=17_000_000_000, bytes_accessed=24_000_000, transcendentals=6_000_000),
    )(head_type, jnp.transpose(qkv, (0, 2, 1, 3)), out_weight)


def solution(mesh):
    n_seq, n_head = mesh.shape["seq"], mesh.shape["head"]
    return jax.shard_map(
        functools.partial(shards, n_seq, n_head, CHUNKS),
        mesh=mesh,
        in_specs=(P(None, "seq", "head", None), P("head"), P("head", None, None)),
        out_specs=P(("seq", "head"), None),
        check_vma=False,
    )
```

time: 286 us -> 143 us (0.50)
  waiting for transfers between devices: 150 us -> 0 us
  Pallas kernels: 0 us -> 139 us
  matrix products: 55 us -> 0 us
  local copies, waits for them, and re-layouts: 42.7 us -> 3.4 us
  starting transfers between devices: 17.9 us -> 0 us
  between operations: 13.5 us -> 0.01 us
  other arithmetic: 7.11 us -> 0 us
    pallas_call x0 -> x1, Pallas kernels: none -> 139 us  [shards(): pl.pallas_call(functools.partial(kernel, n_seq, n_head, chunks), out_shap...]
    reduce_scatter x1 -> x0, waiting for transfers between devices: 99 us -> none  [shards(): lax.psum_scatter(jnp.dot(combined, sorted_weight, preferred_element_type=...]
    all_to_all x2 -> x0, waiting for transfers between devices: 50.5 us -> none  [the longest x1 50.5 us: shards(): lax.all_to_all(sectioned, 'seq', split_axis=2, concat_axis=1, tiled=True)]
    dot_general x4 -> x0, matrix products: 33.8 us -> none  [the longest x1 18 us: shards(): jnp.dot(combined, sorted_weight, preferred_element_type=jnp.float32)]
    gather x3 -> x0, local copies, waits for them, and re-layouts: 23.9 us -> none  [the longest x1 11 us: shards(): jnp.take(out_weight, ranking, axis=0)]
    sub x3 -> x0, matrix products: 21.2 us -> none  [attend(): weights = jnp.exp(attention_logits - highest)]
    all_to_all x2 -> x0, starting transfers between devices: 17.7 us -> none  [the longest x1 9.49 us: shards(): lax.all_to_all(sectioned, 'seq', split_axis=2, concat_axis=1, tiled=True)]
    reshape x2 -> x0, local copies, waits for them, and re-layouts: 7.28 us -> none  [the longest x1 5.72 us: shards(): sectioned = temporal_heads.reshape(3, 1, tokens_here, temp_count, width)]
  transfers between devices with their start and end apart: 3 -> 0, of which waited for: 2 -> 0; matrix products, arithmetic and copies ran while one was open for 19% -> 0% of each run, Pallas kernels for 0% -> 0%
where the time goes in v1:
time: 143 us; the launch traced here: 142 us
  Pallas kernels  139 us (97%)
  local copies, waits for them, and re-layouts  3.4 us (2%)
    pallas_call x1, Pallas kernels, shards(): pl.pallas_call(functools.partial(kernel, n_seq, n_head, chunks), out_shap...  139 us
    unnamed x1, local copies, waits for them, and re-layouts  3.4 us

profile of v1, /device:TPU:1, one launch (start us, length us, event | category | flops | bytes accessed | tf_op | source)
XLA Modules:
  0.0 142.2 jit_solution(864394866239771196)
XLA Ops:
  0.0 138.8 %shard_map.37 = bf16[256,5120]{1,0:T(8,128)(2,1)} custom-call(s32[10]{0:T(128)} %kind_ref.1, bf16[3,10,1024,128]{3,2,1,0:T(8,128)(2,1)} %bitcast.1, bf16[10,128,5120]{2,1,0:T(8,128)(2,1)} %weight_hbm.1), custom_call_target="tpu_custom_call" | custom-call | flops 16999999488 | bytes 24000000 | tf_op jit(solution)/shard_map/pallas_call | solution.py:282
  138.8 3.4 %copy.5 = bf16[256,5120]{1,0:T(8,128)(2,1)} copy(bf16[256,5120]{1,0:T(8,128)(2,1)} %shard_map.37) | data formatting | bytes 5242880

commit v2 on v1

v2 whole, which is shorter than its diff:
```python
import functools
import math

import jax
import jax.numpy as jnp
from jax import lax
from jax.experimental import pallas as pl
from jax.experimental.pallas import tpu as pltpu
from jax.sharding import PartitionSpec as P

MESH = pl.DeviceIdType.MESH
BLOCK = 8
CHUNKS = 8
UNROLL = 1
STREAMS = 2
NEG = -1e30
TICK = (
    ("ring1", 0, 2, 0, 7),
    ("spatial", 0, -1, 0, 7),
    ("ring0", 0, 1, 0, 7),
    ("send", 1, -1, 0, 7),
    ("ring0", 1, 1, 0, 7),
    ("ring2", 1, 4, 0, 7),
    ("temporal", 2, -1, 0, 7),
    ("send", 2, -2, 0, 7),
    ("project", 0, 0, 0, 7),
    ("ring2", 0, 3, 0, 7),
    ("temporal", 0, -1, 0, 7),
    ("project", 1, 0, 0, 7),
    ("temporal", 1, -1, 0, 7),
    ("send", 0, -2, 0, 7),
    ("ring1", 1, 2, 0, 7),
)


def softmax_times(scores, values, factor):
    highest = jnp.max(scores, axis=-1, keepdims=True)
    weights = jnp.exp2((scores - highest) * factor)
    total = jnp.sum(weights, axis=-1, keepdims=True)
    mixed = jnp.dot(weights.astype(jnp.bfloat16), values, preferred_element_type=jnp.float32)
    return mixed / total


def scores_of(queries, keys):
    return lax.dot_general(queries, keys, (((1,), (1,)), ((), ())), preferred_element_type=jnp.float32)


def kernel(
    n_seq, n_head, chunks, kind_ref, qkv_hbm, weight_hbm, out_hbm,
    qkv, weight, packed, arrived, answers, returned, attended, partial, passing, order,
    qkv_sem, weight_sem, there_send, there_recv, back_send, back_recv, ring_send, ring_recv, out_sem,
):
    heads, tokens, width = qkv.shape[1:]
    half = heads // 2
    groups = (half + 1) // 2
    dests = tokens // BLOCK // chunks
    stride = n_seq // dests
    share = tokens // n_head
    rows = share // chunks
    per_owner = rows // BLOCK
    side_columns = weight.shape[2] // 2
    columns = side_columns // STREAMS
    tiles = packed.shape[2]
    factor = width**-0.5 * math.log2(math.e)
    s = lax.axis_index("seq")
    g = lax.axis_index("head")
    side = (lax.rem(g + 1, n_head), lax.rem(g + n_head - 1, n_head))

    def wrapped(i, n):
        return jnp.where(i >= n, i - n, i)

    block = lax.div(s, stride)
    phase = lax.rem(s, stride)

    qkv_copy = pltpu.make_async_copy(qkv_hbm, qkv, qkv_sem)
    weight_copy = pltpu.make_async_copy(weight_hbm, weight, weight_sem)
    qkv_copy.start()

    barrier = pltpu.get_barrier_semaphore()

    def greet(i, _):
        pl.semaphore_signal(barrier, inc=1, device_id={"seq": wrapped(s + i, n_seq), "head": g}, device_id_type=MESH)
        return 0

    lax.fori_loop(1, n_seq, greet, 0)
    for y in side:
        pl.semaphore_signal(barrier, inc=1, device_id={"seq": s, "head": y}, device_id_type=MESH)

    found = [jnp.int32(0), jnp.int32(0)]
    listed = [jnp.int32(0)] * heads
    for i in range(heads):
        temporal = kind_ref[i] == 1
        place = jnp.where(temporal, found[1] + half, found[0])
        for j in range(heads):
            listed[j] = jnp.where(place == j, jnp.int32(i), listed[j])
        found[0] = found[0] + jnp.where(temporal, 0, 1)
        found[1] = found[1] + jnp.where(temporal, 1, 0)
    for j in range(heads):
        order[j] = listed[j]

    def tiles_of(q):
        return pl.ds(3 * q, min(3, tiles - 3 * q))

    def unit(kind, h):
        at = 6 * (h // 2) + 3 * (h % 2) + kind
        return at // 2, at % 2

    def pack(c, q):
        for o in range(n_head):
            of = pl.ds(pl.multiple_of(share * o + rows * c, rows), rows)
            found = {}
            for h in range(2 * q, min(2 * q + 2, half)):
                for kind in range(3):
                    found[unit(kind, h)] = (
                        qkv[kind, order[half + h], of, :].astype(jnp.float32).reshape(per_owner, BLOCK, width)
                    )
            for t in sorted({at[0] for at in found}):
                low = found[t, 0]
                both = jnp.concatenate([low, found.get((t, 1), low)], axis=1)
                packed[c, pl.ds(o * per_owner, per_owner), t] = both.astype(jnp.bfloat16)

    def part_of(tile, upper):
        half_tile = tile.astype(jnp.float32)[:, BLOCK * upper : BLOCK * (upper + 1)]
        return half_tile.reshape(half_tile.shape[0] * BLOCK, width).astype(jnp.bfloat16)

    def is_dest(c):
        return phase == lax.rem(c, stride)

    def send(c, q):
        pack(c, q)
        send_packed(c, q)

    def send_packed(c, q):
        slot = lax.div(c, stride)

        near, dst = lax.rem(c, stride), arrived.at[slot, s, tiles_of(q)]

        def remote(j):
            pltpu.make_async_remote_copy(
                src_ref=packed.at[c, j, tiles_of(q)], dst_ref=dst,
                send_sem=there_send.at[c, q], recv_sem=there_recv.at[slot, q],
                device_id={"seq": j * stride + near, "head": g}, device_id_type=MESH,
            ).start()

        @pl.when(is_dest(c))
        def _():
            pltpu.make_async_copy(packed.at[c, block, tiles_of(q)], dst, there_recv.at[slot, q]).start()

        @pl.when(jnp.logical_not(is_dest(c)))
        def _():
            remote(block)

        def one(i, _):
            remote(wrapped(block + i, dests))
            return 0

        lax.fori_loop(1, dests, one, 0, unroll=UNROLL)

    def temporal(c, q):
        slot = lax.div(c, stride)

        @pl.when(is_dest(c))
        def _():
            whole = arrived.at[slot, :, tiles_of(q)]
            pltpu.make_async_copy(whole, whole, there_recv.at[slot, q]).wait()
            n = n_seq * BLOCK
            same = lax.rem(lax.broadcasted_iota(jnp.int32, (n, n), 0), BLOCK) == lax.rem(
                lax.broadcasted_iota(jnp.int32, (n, n), 1), BLOCK
            )
            done = []
            for h in range(2 * q, min(2 * q + 2, half)):
                queries, keys, values = (
                    part_of(arrived[slot, :, unit(kind, h)[0]], unit(kind, h)[1]) for kind in range(3)
                )
                scores = jnp.where(same, scores_of(queries, keys), NEG)
                done.append(softmax_times(scores, values, factor).reshape(n_seq, BLOCK, width))
            answers[slot, q] = jnp.concatenate([done[0], done[-1]], axis=1).astype(jnp.bfloat16)

            dst = returned.at[c, q, block]
            pltpu.make_async_copy(answers.at[slot, q, s], dst, back_recv.at[c, q]).start()

            def one(i, _):
                to = wrapped(s + i, n_seq)
                pltpu.make_async_remote_copy(
                    src_ref=answers.at[slot, q, to], dst_ref=dst,
                    send_sem=back_send.at[slot, q], recv_sem=back_recv.at[c, q],
                    device_id={"seq": to, "head": g}, device_id_type=MESH,
                ).start()
                return 0

            lax.fori_loop(1, n_seq, one, 0, unroll=UNROLL)

    def spatial(c, _):
        slot = lax.rem(c, 2)
        for h in range(half):
            head = order[h]
            queries = jnp.concatenate(
                [qkv[0, head, pl.ds(pl.multiple_of(share * o + rows * c, rows), rows), :] for o in range(n_head)], axis=0
            )
            attended[slot, :, h * width : (h + 1) * width] = softmax_times(
                scores_of(queries, qkv[1, head]), qkv[2, head], factor
            ).astype(jnp.bfloat16)

    def ring_start(c, d, t, h):
        owner = lax.rem(g + (n_head - 1 if d == 0 else 1), n_head)
        pltpu.make_async_remote_copy(
            src_ref=partial.at[c, d, h, owner] if t == 0 else passing.at[c, d, h, t - 1],
            dst_ref=passing.at[c, d, h, t], send_sem=ring_send.at[c, d, h, t], recv_sem=ring_recv.at[c, d, h, t],
            device_id={"seq": s, "head": side[d]}, device_id_type=MESH,
        ).start()

    def ring_wait(c, d, t, h, sem):
        pltpu.make_async_copy(passing.at[c, d, h, t], passing.at[c, d, h, t], sem.at[c, d, h, t]).wait()

    def project(c, h):
        slot = lax.rem(c, 2)
        if h == 0:
            for q in range(groups):
                pltpu.make_async_copy(returned.at[c, q], returned.at[c, q], back_recv.at[c, q]).wait()
            for i in range(half):
                attended[slot, :, (half + i) * width : (half + i + 1) * width] = part_of(returned[c, i // 2], i % 2)
        step = 256 if columns % 256 == 0 else columns
        for d in range(2):
            for t in range(0, columns, step):
                cols = pl.ds(d * side_columns + h * columns + t, step)
                rows_of = jnp.concatenate([weight[order[i], :, cols] for i in range(heads)], axis=0)
                total = jnp.dot(attended[slot], rows_of, preferred_element_type=jnp.float32)
                partial[c, d, h, :, :, t : t + step] = total.astype(jnp.bfloat16).reshape(n_head, rows, step)
            ring_start(c, d, 0, h)

    def out_copy(c, d, h):
        return pltpu.make_async_copy(
            passing.at[c, d, h, n_head - 2],
            out_hbm.at[pl.ds(pl.multiple_of(rows * c, rows), rows), pl.ds(d * side_columns + h * columns, columns)],
            out_sem.at[c, d, h],
        )

    def ring(t):
        def step(c, h):
            for d in range(2):
                ring_wait(c, d, t, h, ring_recv)
                owner = lax.rem(g + (2 * n_head - 2 - t if d == 0 else 2 + t), n_head)
                total = passing[c, d, h, t].astype(jnp.float32) + partial[c, d, h, owner].astype(jnp.float32)
                passing[c, d, h, t] = total.astype(jnp.bfloat16)
                if t < n_head - 2:
                    ring_start(c, d, t + 1, h)
                else:
                    out_copy(c, d, h).start()

        return step

    does = dict(send=send, temporal=temporal, spatial=spatial, project=project)
    for t in range(n_head - 1):
        does["ring%d" % t] = ring(t)
    lags = [entry[2] for entry in TICK]

    qkv_copy.wait()
    weight_copy.start()
    for q in range(groups):
        pack(jnp.int32(0), q)
    pl.semaphore_wait(barrier, n_seq - 1 + 2)
    for q in range(groups):
        send_packed(jnp.int32(0), q)

    def tick(k, _):
        for what, part, lag, first, last in TICK:
            c = k - lag
            first = 1 if what == "send" and first == 0 else first

            @pl.when(jnp.logical_and(c >= first, c <= last))
            def _(what=what, part=part, c=c):
                does[what](c, part)

        if min(lags) < 0:
            @pl.when(k == -1)
            def _():
                weight_copy.wait()

        return 0

    lax.fori_loop(min(lags), chunks + max(lags), tick, 0)

    def finish(c, _):
        slot = lax.div(c, stride)
        for h in range(STREAMS):
            for d in range(2):
                for t in range(n_head - 1):
                    ring_wait(c, d, t, h, ring_send)
                out_copy(c, d, h).wait()

        @pl.when(is_dest(c))
        def _():
            for q in range(groups):
                few = packed.at[c, pl.ds(0, dests - 1), tiles_of(q)]
                pltpu.make_async_copy(few, few, there_send.at[c, q]).wait()
                most = answers.at[slot, q, pl.ds(0, n_seq - 1)]
                pltpu.make_async_copy(most, most, back_send.at[slot, q]).wait()

        @pl.when(jnp.logical_not(is_dest(c)))
        def _():
            for q in range(groups):
                every = packed.at[c, :, tiles_of(q)]
                pltpu.make_async_copy(every, every, there_send.at[c, q]).wait()

        return 0

    lax.fori_loop(0, chunks, finish, 0)


def shards(n_seq, n_head, chunks, qkv, head_type, out_weight):
    kinds, tokens, heads, width = qkv.shape
    model = out_weight.shape[2]
    half = heads // 2
    groups, tiles = (half + 1) // 2, (3 * half + 1) // 2
    dests = tokens // BLOCK // chunks
    slots = chunks * dests // n_seq
    rows = tokens // n_head // chunks
    part = model // 2 // STREAMS
    bf16 = jnp.bfloat16
    dma = pltpu.SemaphoreType.DMA
    any_ = pl.BlockSpec(memory_space=pl.ANY)
    return pl.pallas_call(
        functools.partial(kernel, n_seq, n_head, chunks),
        out_shape=jax.ShapeDtypeStruct((tokens // n_head, model), bf16),
        in_specs=[pl.BlockSpec(memory_space=pltpu.SMEM), any_, any_],
        out_specs=any_,
        scratch_shapes=[
            pltpu.VMEM((kinds, heads, tokens, width), bf16),
            pltpu.VMEM((heads, width, model), bf16),
            pltpu.VMEM((chunks, dests, tiles, 2 * BLOCK, width), bf16),
            pltpu.VMEM((slots, n_seq, tiles, 2 * BLOCK, width), bf16),
            pltpu.VMEM((slots, groups, n_seq, 2 * BLOCK, width), bf16),
            pltpu.VMEM((chunks, groups, dests, 2 * BLOCK, width), bf16),
            pltpu.VMEM((2, n_head * rows, heads * width), bf16),
            pltpu.VMEM((chunks, 2, STREAMS, n_head, rows, part), bf16),
            pltpu.VMEM((chunks, 2, STREAMS, n_head - 1, rows, part), bf16),
            pltpu.SMEM((heads,), jnp.int32),
            dma,
            dma,
            dma((chunks, groups)),
            dma((slots, groups)),
            dma((slots, groups)),
            dma((chunks, groups)),
            dma((chunks, 2, STREAMS, n_head - 1)),
            dma((chunks, 2, STREAMS, n_head - 1)),
            dma((chunks, 2, STREAMS)),
        ],
        compiler_params=pltpu.CompilerParams(
            collective_id=0, has_side_effects=True, vmem_limit_bytes=62 * 1024 * 1024
        ),
        cost_estimate=pl.CostEstimate(flops=17_000_000_000, bytes_accessed=24_000_000, transcendentals=6_000_000),
    )(head_type, jnp.transpose(qkv, (0, 2, 1, 3)), out_weight)


def solution(mesh):
    n_seq, n_head = mesh.shape["seq"], mesh.shape["head"]
    return jax.shard_map(
        functools.partial(shards, n_seq, n_head, CHUNKS),
        mesh=mesh,
        in_specs=(P(None, "seq", "head", None), P("head"), P("head", None, None)),
        out_specs=P(("seq", "head"), None),
        check_vma=False,
    )
```

time: 143 us -> 125 us (0.87)
  Pallas kernels: 139 us -> 122 us
    pallas_call x1, Pallas kernels: 139 us -> 122 us  [shards(): pl.pallas_call(functools.partial(kernel, n_seq, n_head, chunks), out_shap...]
where the time goes in v2:
time: 125 us
  Pallas kernels  122 us (98%)
  local copies, waits for them, and re-layouts  3.4 us (3%)
    pallas_call x1, Pallas kernels, shards(): pl.pallas_call(functools.partial(kernel, n_seq, n_head, chunks), out_shap...  122 us
    unnamed x1, local copies, waits for them, and re-layouts  3.4 us

profile of v2, /device:TPU:1, one launch (start us, length us, event | category | flops | bytes accessed | tf_op | source)
XLA Modules:
  0.0 125.1 jit_solution(14201617210969158258)
XLA Ops:
  0.0 121.7 %shard_map.37 = bf16[256,5120]{1,0:T(8,128)(2,1)} custom-call(s32[10]{0:T(128)} %kind_ref.1, bf16[3,10,1024,128]{3,2,1,0:T(8,128)(2,1)} %bitcast.1, bf16[10,128,5120]{2,1,0:T(8,128)(2,1)} %weight_hbm.1), custom_call_target="tpu_custom_call" | custom-call | flops 16999999488 | bytes 24000000 | tf_op jit(solution)/shard_map/pallas_call | solution.py:322
  121.7 3.4 %copy.5 = bf16[256,5120]{1,0:T(8,128)(2,1)} copy(bf16[256,5120]{1,0:T(8,128)(2,1)} %shard_map.37) | data formatting | bytes 5242880

commit v3 on v2

--- a/solution.py
+++ b/solution.py
@@ -14,22 +14,34 @@
 UNROLL = 1
 STREAMS = 2
 NEG = -1e30
+START = (
+    ("send_packed", 2, 0),
+    ("send_packed", 0, 0),
+    ("send_packed", 1, 0),
+    ("temporal", 0, 0),
+    ("temporal", 2, 0),
+    ("temporal", 1, 0),
+    ("send", 2, 1),
+    ("send", 1, 1),
+    ("spatial", 0, 0),
+    ("send", 0, 1),
+)
 TICK = (
-    ("ring1", 0, 2, 0, 7),
-    ("spatial", 0, -1, 0, 7),
-    ("ring0", 0, 1, 0, 7),
-    ("send", 1, -1, 0, 7),
-    ("ring0", 1, 1, 0, 7),
-    ("ring2", 1, 4, 0, 7),
-    ("temporal", 2, -1, 0, 7),
-    ("send", 2, -2, 0, 7),
     ("project", 0, 0, 0, 7),
-    ("ring2", 0, 3, 0, 7),
-    ("temporal", 0, -1, 0, 7),
+    ("temporal", 2, -1, 1, 7),
     ("project", 1, 0, 0, 7),
-    ("temporal", 1, -1, 0, 7),
-    ("send", 0, -2, 0, 7),
-    ("ring1", 1, 2, 0, 7),
+    ("ring1", 0, 1, 0, 7),
+    ("send", 2, -2, 2, 7),
+    ("temporal", 1, -1, 1, 7),
+    ("temporal", 0, -1, 1, 7),
+    ("ring2", 0, 6, 0, 7),
+    ("spatial", 0, -1, 1, 7),
+    ("ring0", 0, 0, 0, 7),
+    ("send", 1, -2, 2, 7),
+    ("ring0", 1, 0, 0, 7),
+    ("ring1", 1, 1, 0, 7),
+    ("send", 0, -2, 2, 7),
+    ("ring2", 1, 10, 0, 7),
 )
 
 
@@ -46,9 +58,9 @@
 
 
 def kernel(
-    n_seq, n_head, chunks, kind_ref, qkv_hbm, weight_hbm, out_hbm,
+    n_seq, n_head, chunks, kind_ref, qkv_hbm, weight_hbm, out,
     qkv, weight, packed, arrived, answers, returned, attended, partial, passing, order,
-    qkv_sem, weight_sem, there_send, there_recv, back_send, back_recv, ring_send, ring_recv, out_sem,
+    qkv_sem, weight_sem, there_send, there_recv, back_send, back_recv, ring_send, ring_recv,
 ):
     heads, tokens, width = qkv.shape[1:]
     half = heads // 2
@@ -228,28 +240,23 @@
                 partial[c, d, h, :, :, t : t + step] = total.astype(jnp.bfloat16).reshape(n_head, rows, step)
             ring_start(c, d, 0, h)
 
-    def out_copy(c, d, h):
-        return pltpu.make_async_copy(
-            passing.at[c, d, h, n_head - 2],
-            out_hbm.at[pl.ds(pl.multiple_of(rows * c, rows), rows), pl.ds(d * side_columns + h * columns, columns)],
-            out_sem.at[c, d, h],
-        )
-
     def ring(t):
         def step(c, h):
             for d in range(2):
                 ring_wait(c, d, t, h, ring_recv)
                 owner = lax.rem(g + (2 * n_head - 2 - t if d == 0 else 2 + t), n_head)
                 total = passing[c, d, h, t].astype(jnp.float32) + partial[c, d, h, owner].astype(jnp.float32)
-                passing[c, d, h, t] = total.astype(jnp.bfloat16)
+                total = total.astype(jnp.bfloat16)
                 if t < n_head - 2:
+                    passing[c, d, h, t] = total
                     ring_start(c, d, t + 1, h)
                 else:
-                    out_copy(c, d, h).start()
+                    first = d * side_columns + h * columns
+                    out[pl.ds(pl.multiple_of(rows * c, rows), rows), first : first + columns] = total
 
         return step
 
-    does = dict(send=send, temporal=temporal, spatial=spatial, project=project)
+    does = dict(send=send, send_packed=send_packed, temporal=temporal, spatial=spatial, project=project)
     for t in range(n_head - 1):
         does["ring%d" % t] = ring(t)
     lags = [entry[2] for entry in TICK]
@@ -259,26 +266,20 @@
     for q in range(groups):
         pack(jnp.int32(0), q)
     pl.semaphore_wait(barrier, n_seq - 1 + 2)
-    for q in range(groups):
-        send_packed(jnp.int32(0), q)
+    for what, part, c in START:
+        does[what](jnp.int32(c), part)
+    weight_copy.wait()
 
     def tick(k, _):
         for what, part, lag, first, last in TICK:
             c = k - lag
-            first = 1 if what == "send" and first == 0 else first
-
             @pl.when(jnp.logical_and(c >= first, c <= last))
             def _(what=what, part=part, c=c):
                 does[what](c, part)
 
-        if min(lags) < 0:
-            @pl.when(k == -1)
-            def _():
-                weight_copy.wait()
-
         return 0
 
-    lax.fori_loop(min(lags), chunks + max(lags), tick, 0)
+    lax.fori_loop(0, chunks + max(lags), tick, 0)
 
     def finish(c, _):
         slot = lax.div(c, stride)
@@ -286,7 +287,6 @@
             for d in range(2):
                 for t in range(n_head - 1):
                     ring_wait(c, d, t, h, ring_send)
-                out_copy(c, d, h).wait()
 
         @pl.when(is_dest(c))
         def _():
@@ -321,9 +321,9 @@
     any_ = pl.BlockSpec(memory_space=pl.ANY)
     return pl.pallas_call(
         functools.partial(kernel, n_seq, n_head, chunks),
-        out_shape=jax.ShapeDtypeStruct((tokens // n_head, model), bf16),
+        out_shape=pltpu.VMEM((tokens // n_head, model), bf16),
         in_specs=[pl.BlockSpec(memory_space=pltpu.SMEM), any_, any_],
-        out_specs=any_,
+        out_specs=pl.BlockSpec(memory_space=pltpu.VMEM),
         scratch_shapes=[
             pltpu.VMEM((kinds, heads, tokens, width), bf16),
             pltpu.VMEM((heads, width, model), bf16),
@@ -343,10 +343,9 @@
             dma((chunks, groups)),
             dma((chunks, 2, STREAMS, n_head - 1)),
             dma((chunks, 2, STREAMS, n_head - 1)),
-            dma((chunks, 2, STREAMS)),
         ],
         compiler_params=pltpu.CompilerParams(
-            collective_id=0, has_side_effects=True, vmem_limit_bytes=62 * 1024 * 1024
+            collective_id=0, has_side_effects=True, vmem_limit_bytes=56 * 1024 * 1024
         ),
         cost_estimate=pl.CostEstimate(flops=17_000_000_000, bytes_accessed=24_000_000, transcendentals=6_000_000),
     )(head_type, jnp.transpose(qkv, (0, 2, 1, 3)), out_weight)

time: 125 us -> 121 us (0.968)
  Pallas kernels: 122 us -> 120 us
  local copies, waits for them, and re-layouts: 3.4 us -> 1.49 us
    unnamed x1, local copies, waits for them, and re-layouts: 3.4 us -> 1.49 us
    pallas_call x1, Pallas kernels: 122 us -> 120 us  [shards(): pl.pallas_call(functools.partial(kernel, n_seq, n_head, chunks), out_shap...]
where the time goes in v3:
time: 121 us
  Pallas kernels  120 us (99%)
  local copies, waits for them, and re-layouts  1.49 us (1%)
    pallas_call x1, Pallas kernels, shards(): pl.pallas_call(functools.partial(kernel, n_seq, n_head, chunks), out_shap...  120 us

profile of v3, /device:TPU:1, one launch (start us, length us, event | category | flops | bytes accessed | tf_op | source)
XLA Modules:
  0.0 121.3 jit_solution(11788170585837991100)
XLA Ops:
  0.0 119.8 %shard_map.37 = bf16[256,5120]{1,0:T(8,128)(2,1)S(1)} custom-call(s32[10]{0:T(128)} %kind_ref.1, bf16[3,10,1024,128]{3,2,1,0:T(8,128)(2,1)} %bitcast.1, bf16[10,128,5120]{2,1,0:T(8,128)(2,1)} %weight_hbm.1), custom_call_target="tpu_custom_call" | custom-call | flops 16999999488 | bytes 24000000 | tf_op jit(solution)/shard_map/pallas_call | solution.py:322
  119.8 1.5 %copy.5 = bf16[256,5120]{1,0:T(8,128)(2,1)} copy(bf16[256,5120]{1,0:T(8,128)(2,1)S(1)} %shard_map.37) | data formatting | bytes 5242880

commit v4 on v3

--- a/solution.py
+++ b/solution.py
@@ -18,26 +18,26 @@
     ("send_packed", 2, 0),
     ("send_packed", 0, 0),
     ("send_packed", 1, 0),
+    ("send", 2, 1),
+    ("temporal", 2, 0),
     ("temporal", 0, 0),
-    ("temporal", 2, 0),
     ("temporal", 1, 0),
-    ("send", 2, 1),
+    ("send", 0, 1),
     ("send", 1, 1),
     ("spatial", 0, 0),
-    ("send", 0, 1),
 )
 TICK = (
+    ("temporal", 2, -1, 1, 7),
     ("project", 0, 0, 0, 7),
-    ("temporal", 2, -1, 1, 7),
     ("project", 1, 0, 0, 7),
     ("ring1", 0, 1, 0, 7),
     ("send", 2, -2, 2, 7),
     ("temporal", 1, -1, 1, 7),
     ("temporal", 0, -1, 1, 7),
     ("ring2", 0, 6, 0, 7),
-    ("spatial", 0, -1, 1, 7),
     ("ring0", 0, 0, 0, 7),
     ("send", 1, -2, 2, 7),
+    ("spatial", 0, -1, 1, 7),
     ("ring0", 1, 0, 0, 7),
     ("ring1", 1, 1, 0, 7),
     ("send", 0, -2, 2, 7),
@@ -84,9 +84,9 @@
     block = lax.div(s, stride)
     phase = lax.rem(s, stride)
 
-    qkv_copy = pltpu.make_async_copy(qkv_hbm, qkv, qkv_sem)
     weight_copy = pltpu.make_async_copy(weight_hbm, weight, weight_sem)
-    qkv_copy.start()
+    for kind in range(3):
+        pltpu.make_async_copy(qkv_hbm.at[kind], qkv.at[kind], qkv_sem.at[kind]).start()
 
     barrier = pltpu.get_barrier_semaphore()
 
@@ -261,7 +261,8 @@
         does["ring%d" % t] = ring(t)
     lags = [entry[2] for entry in TICK]
 
-    qkv_copy.wait()
+    for kind in range(3):
+        pltpu.make_async_copy(qkv_hbm.at[kind], qkv.at[kind], qkv_sem.at[kind]).wait()
     weight_copy.start()
     for q in range(groups):
         pack(jnp.int32(0), q)
@@ -335,7 +336,7 @@
             pltpu.VMEM((chunks, 2, STREAMS, n_head, rows, part), bf16),
             pltpu.VMEM((chunks, 2, STREAMS, n_head - 1, rows, part), bf16),
             pltpu.SMEM((heads,), jnp.int32),
-            dma,
+            dma((3,)),
             dma,
             dma((chunks, groups)),
             dma((slots, groups)),

time: 121 us -> 119 us (0.983)
  Pallas kernels: 120 us -> 117 us
    pallas_call x1, Pallas kernels: 120 us -> 117 us  [shards(): pl.pallas_call(functools.partial(kernel, n_seq, n_head, chunks), out_shap...]
where the time goes in v4:
time: 119 us; the launch traced here: 118 us
  Pallas kernels  117 us (98%)
  local copies, waits for them, and re-layouts  1.49 us (1%)
    pallas_call x1, Pallas kernels, shards(): pl.pallas_call(functools.partial(kernel, n_seq, n_head, chunks), out_shap...  117 us

profile of v4, /device:TPU:1, one launch (start us, length us, event | category | flops | bytes accessed | tf_op | source)
XLA Modules:
  0.0 118.5 jit_solution(14610160684991804975)
XLA Ops:
  0.0 117.0 %shard_map.37 = bf16[256,5120]{1,0:T(8,128)(2,1)S(1)} custom-call(s32[10]{0:T(128)} %kind_ref.1, bf16[3,10,1024,128]{3,2,1,0:T(8,128)(2,1)} %bitcast.1, bf16[10,128,5120]{2,1,0:T(8,128)(2,1)} %weight_hbm.1), custom_call_target="tpu_custom_call" | custom-call | flops 16999999488 | bytes 24000000 | tf_op jit(solution)/shard_map/pallas_call | solution.py:323
  117.0 1.5 %copy.5 = bf16[256,5120]{1,0:T(8,128)(2,1)} copy(bf16[256,5120]{1,0:T(8,128)(2,1)S(1)} %shard_map.37) | data formatting | bytes 5242880

commit v5 on v4

--- a/solution.py
+++ b/solution.py
@@ -23,8 +23,8 @@
     ("temporal", 0, 0),
     ("temporal", 1, 0),
     ("send", 0, 1),
+    ("spatial", 0, 0),
     ("send", 1, 1),
-    ("spatial", 0, 0),
 )
 TICK = (
     ("temporal", 2, -1, 1, 7),
@@ -231,7 +231,7 @@
                 pltpu.make_async_copy(returned.at[c, q], returned.at[c, q], back_recv.at[c, q]).wait()
             for i in range(half):
                 attended[slot, :, (half + i) * width : (half + i + 1) * width] = part_of(returned[c, i // 2], i % 2)
-        step = 256 if columns % 256 == 0 else columns
+        step = 640 if columns % 640 == 0 else columns
         for d in range(2):
             for t in range(0, columns, step):
                 cols = pl.ds(d * side_columns + h * columns + t, step)

time: 119 us -> 119 us (level)
  no operation moved by 1% of the time
where the time goes in v5:
time: 119 us; the launch traced here: 118 us
  Pallas kernels  117 us (98%)
  local copies, waits for them, and re-layouts  1.49 us (1%)
    pallas_call x1, Pallas kernels, shards(): pl.pallas_call(functools.partial(kernel, n_seq, n_head, chunks), out_shap...  117 us

profile of v5, /device:TPU:1, one launch (start us, length us, event | category | flops | bytes accessed | tf_op | source)
XLA Modules:
  0.0 118.5 jit_solution(4797347703075191193)
XLA Ops:
  0.0 117.0 %shard_map.37 = bf16[256,5120]{1,0:T(8,128)(2,1)S(1)} custom-call(s32[10]{0:T(128)} %kind_ref.1, bf16[3,10,1024,128]{3,2,1,0:T(8,128)(2,1)} %bitcast.1, bf16[10,128,5120]{2,1,0:T(8,128)(2,1)} %weight_hbm.1), custom_call_target="tpu_custom_call" | custom-call | flops 16999999488 | bytes 24000000 | tf_op jit(solution)/shard_map/pallas_call | solution.py:323
  117.0 1.5 %copy.5 = bf16[256,5120]{1,0:T(8,128)(2,1)} copy(bf16[256,5120]{1,0:T(8,128)(2,1)S(1)} %shard_map.37) | data formatting | bytes 5242880
